TPU v7x, 128 devices: a whole 4x4x4 slice. The times are simulated.
128 devices in a mesh: rows: 32 (over z, y, core), rep: 4 (over x).
Axes of the slice: x: 4, y: 4, z: 4, core: 2. Of those that a mesh axis runs over, the one named last changes fastest.
Arguments:
- item_table: float32 [524288, 128], P('rows'), may hold values from -6 to 6
- item_ids: int32 [32768, 16], P(('rows', 'rep')), may hold values from 0 to 524287, as said below
- ratings: float32 [32768, 16], P(('rows', 'rep')), may hold values from 0.1 to 10
- counts: int32 [32768], P(('rows', 'rep')), may hold values from 1 to 16
- user_batch: int32 [32768], P(('rows', 'rep')), may hold values from 0 to 32767, as said below
Outputs:
- user_table: float32 [32768, 128], P(('rows', 'rep'))
Inputs may be any that keep to these rules, and one draw needn't show every extreme that they name: `item_ids`: each device's 256 x 16 entries name exactly 128 items of every block of 16384 consecutive items, padded entries too. `user_batch`: A permutation of all users; each device's 256 slots hold exactly 2 users of every block of 256 consecutive users.
All inputs are finite; a program needn't handle non-finite values.
Results may differ from a plain program's by a relative error of at most 0.007.
Values sent between devices are 32-bit elements; how exact they have to be, the bound alone decides.
A program may use at most 192 MiB of HBM per device.

v0:
```python
import jax
import jax.numpy as jnp
from jax import lax
from jax.sharding import PartitionSpec as P

ITERS = 8


HIGH = lax.Precision.HIGHEST
REG_WEIGHT = 1.0
GRAM_WEIGHT = 4.0


def solve_users(looked, ratings, counts, scaled):
    length = looked.shape[1]
    live = jnp.arange(length)[None, :] < counts[:, None]
    weight = jnp.where(live, ratings, 0.0)
    pull = jnp.where(live, 1.0 + ratings, 0.0)
    rhs = jnp.einsum("ul,ulk->uk", pull, looked, precision=HIGH)
    solved = jnp.zeros_like(rhs)
    resid = rhs
    direc = rhs
    norm_now = jnp.sum(resid * resid, axis=1, keepdims=True)
    for step in range(ITERS):
        proj = jnp.einsum("ulk,uk->ul", looked, direc, precision=HIGH)
        spread = jnp.einsum("ul,ulk->uk", weight * proj, looked, precision=HIGH)
        image = jnp.dot(direc, scaled, precision=HIGH) + spread + REG_WEIGHT * direc
        alpha = norm_now / jnp.sum(direc * image, axis=1, keepdims=True)
        solved = solved + alpha * direc
        resid = resid - alpha * image
        norm_next = jnp.sum(resid * resid, axis=1, keepdims=True)
        direc = resid + norm_next / norm_now * direc
        norm_now = norm_next
    return solved


def body(item_table, item_ids, ratings, counts, user_batch):
    users, length = item_ids.shape
    shard_rows, width = item_table.shape
    row_count = lax.axis_size("rows")
    rep_count = lax.axis_size("rep")
    first_row = lax.axis_index("rows") * shard_rows
    flat_ids = item_ids.reshape(-1)
    slots = flat_ids.shape[0]
    bucket = slots // row_count
    every_id = lax.all_gather(flat_ids, "rows", axis=0, tiled=True)
    blocks = slots * lax.axis_size("rows") // slots
    local_rows = (every_id - first_row).reshape(blocks, slots)
    owned = (local_rows >= 0) & (local_rows < shard_rows)
    rank = jnp.cumsum(owned.astype(jnp.int32), axis=1) - 1
    select = owned[:, :, None] & (
        rank[:, :, None] == jnp.arange(bucket, dtype=jnp.int32)[None, None, :]
    )
    compact = jnp.sum(jnp.where(select, local_rows[:, :, None], 0), axis=1)
    picked = item_table[compact]
    placed = jnp.einsum("bsj,bjk->bsk", select.astype(jnp.float32), picked, precision=HIGH)
    looked = lax.psum_scatter(
        placed.reshape(slots * lax.axis_size("rows"), width),
        "rows",
        scatter_dimension=0,
        tiled=True,
    )
    looked = looked.reshape(users, length, width)
    gram = lax.psum(jnp.dot(item_table.T, item_table, precision=HIGH), "rows")
    total_items = shard_rows * row_count
    scaled = gram * (GRAM_WEIGHT * width / total_items)
    solved = solve_users(looked, ratings, counts, scaled)
    device_count = row_count * rep_count
    per_owner = users // device_count
    owners = user_batch // users
    order_out = jnp.argsort(owners, stable=True)
    rows_out = solved[order_out]
    ids_out = user_batch[order_out]
    got_rows, got_ids = (
        lax.all_to_all(
            rows_out.reshape(device_count, per_owner, width),
            ("rows", "rep"),
            split_axis=0,
            concat_axis=0,
            tiled=True,
        ),
        lax.all_to_all(
            ids_out.reshape(device_count, per_owner),
            ("rows", "rep"),
            split_axis=0,
            concat_axis=0,
            tiled=True,
        ),
    )
    place = got_ids.reshape(-1) % users
    return jnp.zeros((users, width), jnp.float32).at[place].set(got_rows.reshape(-1, width))


def solution(mesh):
    in_specs = (
        P("rows", None),
        P(("rows", "rep"), None),
        P(("rows", "rep"), None),
        P(("rows", "rep")),
        P(("rows", "rep")),
    )
    out_specs = P(("rows", "rep"), None)
    return jax.shard_map(body, mesh=mesh, in_specs=in_specs, out_specs=out_specs, check_vma=False)
```

profile of v0, /device:TPU:1, one launch (start us, length us, event | category | flops | bytes accessed | tf_op | source)
XLA Modules:
  0.0 627.5 jit_solution(11689296890506217607)
XLA Ops:
  6.5 0.8 copy.10
  7.4 0.1 reshape.233
  7.5 27.6 %all_gather.3 = s32[131072]{0:T(1024)S(1)} all-gather(s32[4096]{0:T(1024)S(1)} %reshape.233), channel_id=1, replica_groups=mesh['rows'=32,'rep'=4] {'rows'}, dimensions={0}, use_global_device_ids=true | all-gather | bytes 540672 | tf_op jit(solution)/shard_map/all_gather | solution.py:46
  35.2 9.2 %reduce-window.6 = s32[32,32,128]{2,1,0:T(8,128)S(1)} reduce-window(s32[32,32,128]{2,1,0:T(8,128)S(1)} %bitcast.66, s32[]{:T(128)} %constant.45.clone.1), window={size=1x1x128 pad=0_0x0_0x127_0}, to_apply=%region_1.2 | reduce-window | flops 16646144 | bytes 1048580 | tf_op jit(solution)/shard_map/reduce-window
  44.4 0.8 slice_reduce_fusion
  45.2 0.2 reduce-window.9
  45.4 0.2 add_add_fusion
  45.6 0.3 copy.154
  45.9 0.1 reshape.234
  46.0 0.1 compare_and_fusion
  46.1 57.0 %select_reduce_fusion = s32[32,128]{1,0:T(8,128)S(1)} fusion(s32[32,4096]{1,0:T(8,128)S(1)} %reshape.234, s32[32,4096]{1,0:T(8,128)S(1)} %bitcast.64, pred[32,4096]{1,0:T(8,128)(4,1)S(1)} %compare_and_fusion), kind=kLoop, calls=%fused_computation.4 | loop fusion | flops 67104768 | bytes 1196032 | tf_op jit(solution)/shard_map/reduce_sum | solution.py:54
  103.1 17.5 %gather_fusion.1 = f32[4096,128]{1,0:T(8,128)} fusion(f32[16384,128]{1,0:T(8,128)} %param.5, s32[4096]{0:T(1024)S(1)} %fusion.34), kind=kCustom, calls=%fused_computation.1 | custom fusion | bytes 4210688 | tf_op jit(solution)/shard_map/gather | solution.py:55
  120.6 68.3 %fusion.1 = f32[32,4096,128]{2,1,0:T(8,128)} fusion(f32[32,128,128]{2,1,0:T(8,128)} %bitcast.68, s32[32,4096]{1,0:T(8,128)S(1)} %bitcast.65, pred[32,4096]{1,0:T(8,128)(4,1)S(1)} %compare_and_fusion), kind=kOutput, calls=%fused_computation.7 | convolution fusion | flops 25803358208 | bytes 69861376 | tf_op jit(solution)/shard_map/bsj,bjk->bsk/dot_general | solution.py:56
  188.9 0.7 copy-done
  189.6 3.2 sort.17
  192.8 1.9 gather_fusion
  194.7 0.8 all_to_all.9
  195.5 7.0 %all-to-all-start = ((s32[128,1,2]{2,1,0:T(1,128)}), s32[128,1,2]{2,1,0:T(1,128)S(1)}, u32[]{:S(2)}, u32[]{:S(2)}) async-start(s32[128,1,2]{2,1,0:T(1,128)} %bitcast.8), calls=%async_computation | async-start | bytes 131072 | tf_op jit(solution)/shard_map/all_to_all | solution.py:82
  202.6 0.2 all-reduce.2.cloned.1.call-start
  202.8 19.8 %fusion.53 = f32[128,128]{1,0:T(8,128)} fusion(f32[16384,128]{1,0:T(8,128)} %param.5), kind=kOutput, calls=%fused_computation.132 | convolution fusion | flops 3221225472 | bytes 8454144 | tf_op jit(solution)/shard_map/dot_general | solution.py:64
  222.7 0.1 copy.89
  222.8 0.5 broadcast.149
  223.3 0.8 reduce.39
  224.1 0.1 reshape.232
  224.3 256.5 %reduce-scatter.2.cloned.1.call-done = f32[4096,128]{1,0:T(8,128)} async-done(((f32[131072,128]{1,0:T(8,128)}), f32[4096,128]{1,0:T(8,128)}) %reduce-scatter.2.cloned.1.call-update) | async-done | bytes 2097168 | tf_op jit(solution)/shard_map/reduce_scatter | solution.py:57
  480.8 2.8 multiply_reduce_fusion.16
  483.5 0.6 multiply_reduce_fusion.15
  484.2 0.1 copy.97
  484.3 1.4 multiply_reduce_fusion.14
  485.9 0.1 copy.25
  486.0 93.2 %all-reduce.2.cloned.1.call-done = f32[128,128]{1,0:T(8,128)} async-done(((f32[128,128]{1,0:T(8,128)}), f32[128,128]{1,0:T(8,128)}) %all-reduce.2.cloned.1.call-update) | async-done | bytes 65552 | tf_op jit(solution)/shard_map/psum | solution.py:64
  579.2 1.2 multiply_reduce_fusion.30
  580.6 0.6 multiply_reduce_fusion.13
  581.3 0.1 copy.104
  581.4 1.6 multiply_reduce_fusion.12
  583.1 0.3 multiply_reduce_fusion.28
  583.7 0.6 multiply_reduce_fusion.11
  584.4 0.1 copy.111
  584.5 1.4 multiply_reduce_fusion.10
  586.0 0.3 multiply_reduce_fusion.26
  586.6 0.6 multiply_reduce_fusion.9
  587.3 0.1 copy.118
  587.4 1.4 multiply_reduce_fusion.8
  588.9 0.3 multiply_reduce_fusion.24
  589.4 0.6 multiply_reduce_fusion.7
  590.1 0.1 copy.125
  590.2 1.4 multiply_reduce_fusion.6
  591.8 0.3 multiply_reduce_fusion.22
  592.3 0.6 multiply_reduce_fusion.5
  593.0 0.1 copy.132
  593.1 1.4 multiply_reduce_fusion.4
  594.6 0.3 multiply_reduce_fusion.20
  595.2 0.6 multiply_reduce_fusion.3
  595.9 0.1 copy.139
  596.0 1.4 multiply_reduce_fusion.2
  597.5 0.3 multiply_reduce_fusion.18
  598.0 0.6 multiply_reduce_fusion.1
  598.7 0.1 copy.145
  598.9 1.4 multiply_reduce_fusion
  600.4 0.3 fusion.14
  600.9 1.3 gather_fusion.2
  602.3 6.8 %all-to-all-start.1 = ((f32[128,2,128]{2,1,0:T(2,128)}), f32[128,2,128]{2,1,0:T(2,128)S(1)}, u32[]{:S(2)}, u32[]{:S(2)}) async-start(f32[128,2,128]{2,1,0:T(2,128)} %bitcast.24), calls=%async_computation.2 | async-start | bytes 262144 | tf_op jit(solution)/shard_map/all_to_all | solution.py:75
  609.1 9.8 %all-to-all-done.1 = f32[128,2,128]{2,1,0:T(2,128)S(1)} async-done(((f32[128,2,128]{2,1,0:T(2,128)}), f32[128,2,128]{2,1,0:T(2,128)S(1)}, u32[]{:S(2)}, u32[]{:S(2)}) %all-to-all-start.1) | async-done | bytes 131104 | tf_op jit(solution)/shard_map/all_to_all | solution.py:75
  618.9 1.8 scatter_custom_fusion
  (83 shorter events, 2.8 us)
Async XLA Ops:
  6.5 474.2 %reduce-scatter.2.cloned.1.call-start = ((), (), s32[]{:S(2)}) async-start(), calls=%async_computation.3 | async-start | bytes 69206016 | tf_op jit(solution)/shard_map/reduce_scatter | solution.py:57
  188.9 0.7 copy-start
  195.5 27.3 %all-to-all-start = ((s32[128,1,2]{2,1,0:T(1,128)}), s32[128,1,2]{2,1,0:T(1,128)S(1)}, u32[]{:S(2)}, u32[]{:S(2)}) async-start(s32[128,1,2]{2,1,0:T(1,128)} %bitcast.8), calls=%async_computation | async-start | bytes 131072 | tf_op jit(solution)/shard_map/all_to_all | solution.py:82
  202.5 20.1 %copy-start.3 = (f32[256,16]{0,1:T(8,128)S(1)}, f32[256,16]{0,1:T(8,128)}, u32[]{:S(2)}) copy-start(f32[256,16]{0,1:T(8,128)} %param.7) | copy-start | bytes 49156
  202.5 20.1 %copy-start.4 = (s32[256]{0:T(256)S(1)}, s32[256]{0:T(256)}, u32[]{:S(2)}) copy-start(s32[256]{0:T(256)} %param.8) | copy-start | bytes 3076
  202.6 376.6 %all-reduce.2.cloned.1.call-start = ((), (), s32[]{:S(2)}) async-start(), calls=%async_computation.4 | async-start | bytes 131072 | tf_op jit(solution)/shard_map/psum | solution.py:64
  480.8 2.8 copy-start.1
  580.6 2.6 copy-start.2
  602.3 16.6 %all-to-all-start.1 = ((f32[128,2,128]{2,1,0:T(2,128)}), f32[128,2,128]{2,1,0:T(2,128)S(1)}, u32[]{:S(2)}, u32[]{:S(2)}) async-start(f32[128,2,128]{2,1,0:T(2,128)} %bitcast.24), calls=%async_computation.2 | async-start | bytes 262144 | tf_op jit(solution)/shard_map/all_to_all | solution.py:75
Sparse Core Ops, SparseCore 0:
  189.1 291.6 reduce-scatter.1
  484.0 95.1 all-reduce.1
where the time goes:
time: 628 us
  waiting for transfers between devices  360 us (57%)
  matrix products  91.7 us (15%)
  other arithmetic  90.8 us (14%)
  local copies, waits for them, and re-layouts  29.7 us (5%)
  blocking collectives  27.6 us (4%)
  between operations  14.1 us (2%)
  starting transfers between devices  14 us (2%)
    reduce_scatter x1, waiting for transfers between devices, body(): lax.psum_scatter(placed.reshape(slots * lax.axis_size('rows'), width), 'r...  256 us
    psum x1, waiting for transfers between devices, body(): gram = lax.psum(jnp.dot(item_table.T, item_table, precision=HIGH), 'rows')  93.2 us
    dot_general x1, matrix products, body(): jnp.einsum('bsj,bjk->bsk', select.astype(jnp.float32), picked, precision=...  68.3 us
    reduce_sum x1, other arithmetic, body(): compact = jnp.sum(jnp.where(select, local_rows[:, :, None], 0), axis=1)  57 us
    all_gather x1, blocking collectives, body(): every_id = lax.all_gather(flat_ids, 'rows', axis=0, tiled=True)  27.6 us
    dot_general x1, matrix products, body(): gram = lax.psum(jnp.dot(item_table.T, item_table, precision=HIGH), 'rows')  19.8 us
    gather x1, local copies, waits for them, and re-layouts, body(): picked = item_table[compact]  17.5 us
    unnamed x16, other arithmetic  16.5 us
  transfers between devices with their start and end apart: 4, of which 3 were waited for; matrix products, arithmetic and copies ran while one was open for 5% of the time, Pallas kernels for 0%

commit v1 on v0

v1 whole, which is shorter than its diff:
```python
import functools

import jax
import jax.numpy as jnp
from jax import lax
from jax.experimental import pallas as pl
from jax.experimental.pallas import tpu as pltpu
from jax.sharding import PartitionSpec as P

ITERS = 8
REG_WEIGHT = 1.0
GRAM_WEIGHT = 4.0
HIGH = lax.Precision.HIGHEST
MESH = pl.DeviceIdType.MESH

IDS, ROWS, GRAM_X, PLACE_X, GRAM_SUM, PLACE_ROWS, GRAM_ALL, GRAM_BACK, OUT_X, OUT_ROWS = range(10)


def ring_steps(rows):
    def hops(d):
        dy, dz = (d // 2) % 4, d // 8
        return min(dy, 4 - dy) + min(dz, 4 - dz)

    return sorted(range(1, rows), key=lambda d: (-hops(d), d % 2))


def shifted(me, d):
    c, y, z = me % 2, (me // 2) % 4, me // 8
    dc, dy, dz = d % 2, (d // 2) % 4, d // 8
    return ((z + dz) % 4 * 4 + (y + dy) % 4) * 2 + (c + dc) % 2


def dot(a, b, dims, precision=HIGH):
    return lax.dot_general(a, b, (dims, ((), ())), precision=precision, preferred_element_type=jnp.float32)


def iota(shape, axis):
    return lax.broadcasted_iota(jnp.int32, shape, axis)


def kernel(
    rows, reps, ids_ref, rat_ref, cnt_ref, ub_ref, table_ref, out_ref,
    tv, sendb, recvb, lt, blk, cid, rid, rid_s, pos_v, pos_s,
    gpart, gx, g1, gr, g2, gfull, smat,
    place_a, place_b, place_c, place_d, hot_out, out_a, out_b, out_c, out_d,
    w_s, q_s, x_s, r_s, p_s, ssem, rsem, lsem,
):
    me = lax.axis_index("rows")
    rep = lax.axis_index("rep")
    items = tv.shape[0]
    length, users = ids_ref.shape
    width = tv.shape[1]
    bucket = users * length // rows
    quarter = items // reps
    halves = users // width
    steps = ring_steps(rows)

    def step_of(i):
        d = jnp.int32(steps[0])
        for k in range(1, len(steps)):
            d = jnp.where(i == k, steps[k], d)
        return d

    def table_part(q):
        at = pl.multiple_of(lax.rem(rep + q, reps) * quarter, quarter)
        return pltpu.make_async_copy(table_ref.at[pl.ds(at, quarter)], tv.at[pl.ds(at, quarter)], lsem.at[q])

    for q in range(reps):
        table_part(q).start()

    barrier = pltpu.get_barrier_semaphore()

    def greet(d, c):
        pl.semaphore_signal(barrier, 1, device_id={"rows": shifted(me, d)}, device_id_type=MESH)
        return c

    lax.fori_loop(1, rows, greet, 0)
    for q in range(1, reps):
        pl.semaphore_signal(barrier, 1, device_id={"rep": lax.rem(rep + q, reps)}, device_id_type=MESH)

    ids = jnp.concatenate([ids_ref[:, pl.ds(h * width, width)] for h in range(halves)], axis=0)
    owner = ids // items
    local = ids % items
    local_hi = (local // 128).astype(jnp.float32)
    local_lo = (local % 128).astype(jnp.float32)
    lines = ids.shape[0]
    bucket_id = iota((rows, width), 0)
    hits = [(owner[i:i + 1] == bucket_id).astype(jnp.float32) for i in range(lines)]
    before = (iota((width, width), 0) < iota((width, width), 1)).astype(jnp.float32)
    counter = jnp.concatenate([before, jnp.ones((width, width), jnp.float32)], axis=1).astype(jnp.bfloat16)
    counted = dot(jnp.concatenate(hits, axis=0).astype(jnp.bfloat16), counter, ((1,), (0,)), None)
    seen = jnp.zeros((rows, width), jnp.float32)
    ranks = []
    for i in range(lines):
        part = counted[i * rows:(i + 1) * rows]
        ranks.append(jnp.sum(hits[i] * (part[:, :width] + seen), axis=0, keepdims=True))
        seen = seen + part[:, width:]
    rank = jnp.concatenate(ranks, axis=0).astype(jnp.int32)
    pos_v[...] = jnp.clip(owner * bucket + rank, 0, users * length - 1)
    pltpu.make_async_copy(pos_v, pos_s, lsem.at[reps]).start()
    values = jnp.concatenate([jnp.concatenate([hits[i] * local_hi[i:i + 1], hits[i] * local_lo[i:i + 1]], axis=0) for i in range(lines)], axis=1)
    slots = iota((bucket, width), 0)
    picks = jnp.concatenate([(rank[i:i + 1] == slots).astype(jnp.float32) for i in range(lines)], axis=1)
    compact = dot(values.astype(jnp.bfloat16), picks.astype(jnp.bfloat16), ((1,), (1,)), None)
    compact = jnp.clip((compact[:rows] * 128.0 + compact[rows:]).astype(jnp.int32), 0, items - 1)
    for b in range(rows):
        cid[b] = compact[b:b + 1]

    pl.semaphore_wait(barrier, rows - 1 + reps - 1)

    def to_row(t, src, dst, which):
        return pltpu.make_async_remote_copy(
            src_ref=src, dst_ref=dst, send_sem=ssem.at[which], recv_sem=rsem.at[which],
            device_id={"rows": t}, device_id_type=MESH)

    def to_rep(q, src, dst, which):
        return pltpu.make_async_remote_copy(
            src_ref=src, dst_ref=dst, send_sem=ssem.at[which], recv_sem=rsem.at[which],
            device_id={"rep": q}, device_id_type=MESH)

    def each_row(fn):
        def go(i, c):
            fn(shifted(me, step_of(i)))
            return c

        lax.fori_loop(0, rows - 1, go, 0)

    def each_rep(fn):
        for q in range(1, reps):
            fn(lax.rem(rep + q, reps))

    def drain(sem, ref):
        pltpu.make_async_copy(ref, ref, sem).wait()

    each_row(lambda t: to_row(t, cid.at[t], rid.at[me], IDS).start())
    rid[me] = cid[me]
    for q in range(reps):
        table_part(q).wait()
    drain(rsem.at[IDS], rid.at[pl.ds(0, rows - 1)])
    rid[...] = jnp.clip(rid[...], 0, items - 1)
    ids_copy = pltpu.make_async_copy(rid, rid_s, lsem.at[reps + 1])
    ids_copy.start()
    ids_copy.wait()

    def fetch(t, dst, base):
        for k in range(bucket):
            dst[pl.ds(base + k, 1), :] = tv[pl.ds(rid_s[t, 0, k], 1), :]

    def serve(t):
        base = pl.multiple_of(t * bucket, bucket)
        fetch(t, sendb, base)
        at = pl.multiple_of(me * bucket, bucket)
        to_row(t, sendb.at[pl.ds(base, bucket)], recvb.at[pl.ds(at, bucket)], ROWS).start()

    each_row(serve)
    fetch(me, recvb, pl.multiple_of(me * bucket, bucket))

    share = quarter // 8

    def add_gram(i, total):
        part = tv[pl.ds(pl.multiple_of(rep * quarter + i * share, share), share), :]
        return total + dot(part, part, ((0,), (0,)))

    gpart[...] = lax.fori_loop(0, 8, add_gram, jnp.zeros((width, width), jnp.float32))
    chunk = width // reps

    def chunk_of(q):
        return pl.ds(pl.multiple_of(q * chunk, chunk), chunk)

    each_rep(lambda q: to_rep(q, gpart.at[chunk_of(q)], gx.at[chunk_of(rep)], GRAM_X).start())
    gx[chunk_of(rep), :] = gpart[chunk_of(rep), :]

    ub = ub_ref[...]
    home = ub // users
    home_b = jnp.broadcast_to(home, (users, users))
    home_c = jnp.transpose(home_b)
    earlier = iota((users, users), 0) < iota((users, users), 1)
    twin = jnp.sum(jnp.where(earlier & (home_b == home_c), 1.0, 0.0), axis=0, keepdims=True).astype(jnp.int32)
    per_rep = users // reps
    leave = (home % reps) * per_rep + twin * rows + home // reps
    hot = (iota((users, users), 0) == leave).astype(jnp.float32)
    hot_out[...] = hot
    place = jnp.sum(hot * (ub % users).astype(jnp.float32), axis=1, keepdims=True)
    place_a[...] = jnp.broadcast_to(place, (users, width))

    def block_of(q):
        return pl.ds(pl.multiple_of(q * per_rep, per_rep), per_rep)

    def leave_x(a, b, which):
        each_rep(lambda q: to_rep(q, a.at[block_of(q)], b.at[block_of(rep)], which).start())
        b[block_of(rep), :] = a[block_of(rep), :]
        drain(rsem.at[which], b.at[pl.ds(0, users - per_rep)])

    pieces = users // rows

    def piece_of(t):
        return pl.ds(pl.multiple_of(t * pieces, pieces), pieces)

    def leave_rows(b, c, d, which):
        for t in range(rows):
            for j in range(pieces):
                at = t * pieces + j
                c[at:at + 1, :] = b[j * rows + t:j * rows + t + 1, :]
        each_row(lambda t: to_row(t, c.at[piece_of(t)], d.at[piece_of(me)], which).start())
        d[piece_of(me), :] = c[piece_of(me), :]

    def arrived(d, which):
        drain(rsem.at[which], d.at[pl.ds(0, users - pieces)])

    leave_x(place_a, place_b, PLACE_X)
    leave_rows(place_b, place_c, place_d, PLACE_ROWS)

    drain(rsem.at[GRAM_X], gx.at[pl.ds(0, width - chunk)])
    total = gx[0:chunk, :]
    for q in range(1, reps):
        total = total + gx[q * chunk:(q + 1) * chunk, :]
    for b in range(rows):
        g1[b] = total[b:b + 1]
    each_row(lambda t: to_row(t, g1.at[t], gr.at[me], GRAM_SUM).start())
    gr[me] = g1[me]
    drain(rsem.at[GRAM_SUM], gr.at[pl.ds(0, rows - 1)])
    g2[0] = jnp.sum(gr[...], axis=0)
    each_row(lambda t: to_row(t, g2.at[0], gfull.at[rep, me], GRAM_ALL).start())
    gfull[rep, me] = g2[0]
    drain(rsem.at[GRAM_ALL], gr.at[pl.ds(0, rows - 1)])
    each_rep(lambda q: to_rep(q, gfull.at[rep], gfull.at[rep], GRAM_BACK).start())
    drain(rsem.at[GRAM_BACK], gfull.at[pl.ds(0, reps - 1)])
    scale = GRAM_WEIGHT * width / (items * rows)
    for q in range(reps):
        for b in range(rows):
            smat[q * chunk + b:q * chunk + b + 1, :] = gfull[q, b] * scale
    eye = (iota((width, width), 0) == iota((width, width), 1)).astype(jnp.float32)
    smat[...] = smat[...] + REG_WEIGHT * eye

    arrived(place_d, PLACE_ROWS)
    place = place_d[...].astype(jnp.int32)
    back = jnp.concatenate([(place == iota((users, width), 1) + h * width).astype(jnp.float32) for h in range(halves)], axis=1)

    live = iota((length, users), 0) < cnt_ref[...]
    w_s[...] = jnp.where(live, rat_ref[...], 0.0)
    pulls = jnp.where(live, 1.0 + rat_ref[...], 0.0)
    x_s[...] = jnp.zeros_like(x_s)

    pltpu.make_async_copy(pos_v, pos_s, lsem.at[reps]).wait()
    drain(rsem.at[ROWS], recvb.at[pl.ds(0, (rows - 1) * bucket)])

    def turn(i, c):
        for k in range(width):
            blk[pl.ds(k, 1), :] = recvb[pl.ds(pos_s[i, k], 1), :]
        lt[i] = jnp.transpose(blk[...])
        return c

    lax.fori_loop(0, lines, turn, 0)

    for h in range(halves):
        half = slice(h * width, (h + 1) * width)
        rhs = jnp.zeros((width, width), jnp.float32)
        for l in range(length):
            rhs = rhs + lt[h * length + l] * pulls[l:l + 1, half]
        r_s[:, half] = rhs
        p_s[:, half] = rhs

    def iterate(i, norms):
        q_s[...] = dot(smat[...], p_s[...], ((1,), (0,)))
        out = []
        for h in range(halves):
            half = slice(h * width, (h + 1) * width)
            direc = p_s[:, half]
            image = q_s[:, half]
            for l in range(length):
                rows_l = lt[h * length + l]
                proj = jnp.sum(rows_l * direc, axis=0, keepdims=True)
                image = image + rows_l * (w_s[l:l + 1, half] * proj)
            alpha = norms[h] / jnp.sum(direc * image, axis=0, keepdims=True)
            x_s[:, half] = x_s[:, half] + alpha * direc
            resid = r_s[:, half] - alpha * image
            r_s[:, half] = resid
            norm_next = jnp.sum(resid * resid, axis=0, keepdims=True)
            p_s[:, half] = resid + norm_next / norms[h] * direc
            out.append(norm_next)
        return tuple(out)

    start = []
    for h in range(halves):
        first = r_s[:, h * width:(h + 1) * width]
        start.append(jnp.sum(first * first, axis=0, keepdims=True))
    lax.fori_loop(0, ITERS, iterate, tuple(start))

    out_a[...] = dot(hot_out[...], x_s[...], ((1,), (1,)))
    leave_x(out_a, out_b, OUT_X)
    leave_rows(out_b, out_c, out_d, OUT_ROWS)
    arrived(out_d, OUT_ROWS)
    out_ref[...] = dot(back, out_d[...], ((0,), (0,)))

    drain(ssem.at[IDS], rid.at[pl.ds(0, rows - 1)])
    drain(ssem.at[ROWS], sendb.at[pl.ds(0, (rows - 1) * bucket)])
    drain(ssem.at[GRAM_X], gx.at[pl.ds(0, width - chunk)])
    drain(ssem.at[GRAM_SUM], gr.at[pl.ds(0, rows - 1)])
    drain(ssem.at[GRAM_ALL], gr.at[pl.ds(0, rows - 1)])
    drain(ssem.at[GRAM_BACK], gfull.at[pl.ds(0, reps - 1)])
    drain(ssem.at[PLACE_X], place_b.at[pl.ds(0, users - per_rep)])
    drain(ssem.at[PLACE_ROWS], place_d.at[pl.ds(0, users - pieces)])
    drain(ssem.at[OUT_X], out_b.at[pl.ds(0, users - per_rep)])
    drain(ssem.at[OUT_ROWS], out_d.at[pl.ds(0, users - pieces)])


def body(rows, reps, item_table, item_ids, ratings, counts, user_batch):
    users, length = item_ids.shape
    items, width = item_table.shape
    slots = users * length
    f32, i32 = jnp.float32, jnp.int32
    vmem = pl.BlockSpec(memory_space=pltpu.VMEM)
    square = pltpu.VMEM((width, width), f32)
    wide = pltpu.VMEM((width, users), f32)
    tall = pltpu.VMEM((users, width), f32)
    return pl.pallas_call(
        functools.partial(kernel, rows, reps),
        out_shape=jax.ShapeDtypeStruct((users, width), f32),
        in_specs=[vmem] * 4 + [pl.BlockSpec(memory_space=pl.ANY)],
        out_specs=vmem,
        scratch_shapes=[
            pltpu.VMEM((items, width), f32),
            pltpu.VMEM((slots, width), f32),
            pltpu.VMEM((slots, width), f32),
            pltpu.VMEM((slots // width, width, width), f32),
            square,
            pltpu.VMEM((rows, 1, width), i32),
            pltpu.VMEM((rows, 1, width), i32),
            pltpu.SMEM((rows, 1, width), i32),
            pltpu.VMEM((slots // width, width), i32),
            pltpu.SMEM((slots // width, width), i32),
            square,
            square,
            pltpu.VMEM((rows, 1, width), f32),
            pltpu.VMEM((rows, 1, width), f32),
            pltpu.VMEM((1, 1, width), f32),
            pltpu.VMEM((reps, rows, 1, width), f32),
            square,
            tall, tall, tall, tall,
            pltpu.VMEM((users, users), f32),
            tall, tall, tall, tall,
            pltpu.VMEM((length, users), f32),
            wide, wide, wide, wide,
            pltpu.SemaphoreType.DMA((10,)),
            pltpu.SemaphoreType.DMA((10,)),
            pltpu.SemaphoreType.DMA((reps + 2,)),
        ],
        compiler_params=pltpu.CompilerParams(
            collective_id=0, has_side_effects=True, vmem_limit_bytes=40 << 20
        ),
    )(item_ids.T, ratings.T, counts.reshape(1, users), user_batch.reshape(1, users), item_table)


def solution(mesh):
    in_specs = (
        P("rows", None),
        P(("rows", "rep"), None),
        P(("rows", "rep"), None),
        P(("rows", "rep")),
        P(("rows", "rep")),
    )
    out_specs = P(("rows", "rep"), None)
    step = functools.partial(body, mesh.shape["rows"], mesh.shape["rep"])
    return jax.shard_map(step, mesh=mesh, in_specs=in_specs, out_specs=out_specs, check_vma=False)
```

time: 628 us -> 80.3 us (0.13)
  waiting for transfers between devices: 360 us -> 0 us
  matrix products: 91.7 us -> 0 us
  other arithmetic: 90.8 us -> 0 us
  Pallas kernels: 0 us -> 73.1 us
  blocking collectives: 27.6 us -> 0 us
  local copies, waits for them, and re-layouts: 29.7 us -> 6.83 us
  between operations: 14.1 us -> 0.01 us
  starting transfers between devices: 14 us -> 0 us
    reduce_scatter x1 -> x0, waiting for transfers between devices: 256 us -> none  [body(): lax.psum_scatter(placed.reshape(slots * lax.axis_size('rows'), width), 'r...]
    psum x1 -> x0, waiting for transfers between devices: 93.2 us -> none  [body(): gram = lax.psum(jnp.dot(item_table.T, item_table, precision=HIGH), 'rows')]
    dot_general x10 -> x0, matrix products: 91.7 us -> none  [the longest x1 68.3 us: body(): jnp.einsum('bsj,bjk->bsk', select.astype(jnp.float32), picked, precision=...]
    pallas_call x0 -> x1, Pallas kernels: none -> 73.1 us  [body(): pl.pallas_call(functools.partial(kernel, rows, reps), out_shape=jax.Shape...]
    reduce_sum x8 -> x0, other arithmetic: 57.3 us -> none  [the longest x1 57 us: body(): compact = jnp.sum(jnp.where(select, local_rows[:, :, None], 0), axis=1)]
    all_gather x1 -> x0, blocking collectives: 27.6 us -> none  [body(): every_id = lax.all_gather(flat_ids, 'rows', axis=0, tiled=True)]
    gather x3 -> x0, local copies, waits for them, and re-layouts: 20.8 us -> none  [the longest x1 17.5 us: body(): picked = item_table[compact]]
    unnamed x16 -> x0, other arithmetic: 16.5 us -> none
  transfers between devices with their start and end apart: 4 -> 0, of which waited for: 3 -> 0; matrix products, arithmetic and copies ran while one was open for 5% -> 0% of each run, Pallas kernels for 0% -> 0%
where the time goes in v1:
time: 80.3 us; the launch traced here: 80 us
  Pallas kernels  73.1 us (91%)
  local copies, waits for them, and re-layouts  6.83 us (9%)
    pallas_call x1, Pallas kernels, body(): pl.pallas_call(functools.partial(kernel, rows, reps), out_shape=jax.Shape...  73.1 us
    unnamed x11, local copies, waits for them, and re-layouts  6.83 us

profile of v1, /device:TPU:1, one launch (start us, length us, event | category | flops | bytes accessed | tf_op | source)
XLA Modules:
  0.0 80.0 jit_solution(4987628350616382459)
XLA Ops:
  0.0 0.0 copy-start
  0.0 3.4 %copy-done = f32[16384,128]{1,0:T(8,128)S(1)} copy-done((f32[16384,128]{1,0:T(8,128)S(1)}, f32[16384,128]{1,0:T(8,128)}, u32[]{:S(2)}) %copy-start) | copy-done | bytes 8388632
  3.4 0.0 copy-start.1
  3.4 0.7 copy-done.1
  4.1 0.0 copy-start.2
  4.1 0.7 copy-done.2
  4.8 0.0 copy-start.3
  4.8 0.7 copy-done.3
  5.5 0.0 copy-start.4
  5.5 0.7 copy-done.4
  6.2 73.1 %shard_map.55 = f32[256,128]{1,0:T(8,128)S(1)} custom-call(s32[16,256]{1,0:T(8,128)S(1)} %bitcast.4, f32[16,256]{1,0:T(8,128)S(1)} %bitcast.5, s32[1,256]{1,0:T(1,128)S(1)} %bitcast.6, s32[1,256]{1,0:T(1,128)S(1)} %bitcast.7, f32[16384,128]{1,0:T(8,128)S(1)} %copy-done), custom_call_target="tpu_custom_call" | custom-call | tf_op jit(solution)/shard_map/pallas_call | solution.py:316
  79.3 0.7 copy.7
Async XLA Ops:
  0.0 3.4 %copy-start = (f32[16384,128]{1,0:T(8,128)S(1)}, f32[16384,128]{1,0:T(8,128)}, u32[]{:S(2)}) copy-start(f32[16384,128]{1,0:T(8,128)} %table_ref.1) | copy-start | bytes 25165828
  3.4 0.7 copy-start.1
  4.1 0.7 copy-start.2
  4.8 0.7 copy-start.3
  5.5 0.7 copy-start.4

commit v2 on v1

v2 whole, which is shorter than its diff:
```python
import functools

import jax
import jax.numpy as jnp
from jax import lax
from jax.experimental import pallas as pl
from jax.experimental.pallas import tpu as pltpu
from jax.sharding import PartitionSpec as P

ITERS = 8
REG_WEIGHT = 1.0
GRAM_WEIGHT = 4.0
HIGH = lax.Precision.HIGHEST
MESH = pl.DeviceIdType.MESH

ROWS, GRAM_X, PLACE_NEAR, GRAM_SUM, PLACE_FAR, GRAM_ALL, GRAM_BACK, OUT_NEAR, OUT_FAR = range(9)


def ring_steps(rows):
    def hops(d):
        dy, dz = (d // 2) % 4, d // 8
        return min(dy, 4 - dy) + min(dz, 4 - dz)

    return sorted(range(1, rows), key=lambda d: (-hops(d), d % 2))


def opposite(d):
    return (4 - d // 8) % 4 * 8 + (4 - d // 2 % 4) % 4 * 2 + d % 2


def shifted(me, d):
    c, y, z = me % 2, (me // 2) % 4, me // 8
    dc, dy, dz = d % 2, (d // 2) % 4, d // 8
    return ((z + dz) % 4 * 4 + (y + dy) % 4) * 2 + (c + dc) % 2


def dot(a, b, dims, precision=HIGH):
    return lax.dot_general(a, b, (dims, ((), ())), precision=precision, preferred_element_type=jnp.float32)


def iota(shape, axis):
    return lax.broadcasted_iota(jnp.int32, shape, axis)


def kernel(
    rows, reps, ids_hbm, rat_hbm, cnt_hbm, ub_hbm, table_ref, out_hbm,
    ids_ref, rat_ref, cnt_ref, ub_ref, out_ref, tv, sendb, recvb, lt, blk_a, blk_b, cid, rid, rid_s, pos_v, pos_s,
    gpart, gx, g1, gr, g2, gfull, smat,
    place_a, place_b, place_c, place_d, inv_v, inv_s, pull_s, out_a, out_b, out_c, out_d,
    w_s, q_s, x_s, r_s, p_s, ssem, rsem, id_ssem, id_rsem, lsem,
):
    me = lax.axis_index("rows")
    rep = lax.axis_index("rep")
    items = tv.shape[0]
    length, users = ids_ref.shape
    width = tv.shape[1]
    bucket = users * length // rows
    quarter = items // reps
    halves = users // width
    steps = ring_steps(rows)

    def step_of(i):
        d = jnp.int32(steps[0])
        for k in range(1, len(steps)):
            d = jnp.where(i == k, steps[k], d)
        return d

    def table_part(q):
        at = pl.multiple_of(lax.rem(rep + q, reps) * quarter, quarter)
        return pltpu.make_async_copy(table_ref.at[pl.ds(at, quarter)], tv.at[pl.ds(at, quarter)], lsem.at[q])

    small = [
        pltpu.make_async_copy(src, dst, lsem.at[reps + 2 + i])
        for i, (src, dst) in enumerate(((ids_hbm, ids_ref), (rat_hbm, rat_ref), (cnt_hbm, cnt_ref), (ub_hbm, ub_ref)))
    ]
    for copy in small:
        copy.start()
    for q in range(reps):
        table_part(q).start()

    barrier = pltpu.get_barrier_semaphore()

    def next_row(i):
        t = me + i
        return jnp.where(t >= rows, t - rows, t)

    def greet(i, c):
        pl.semaphore_signal(barrier, 1, device_id={"rows": next_row(i)}, device_id_type=MESH)
        return c

    lax.fori_loop(1, rows, greet, 0)
    near = 2 * reps
    core = me % 2
    here = core * reps + rep

    def near_peer(i):
        g = lax.rem(here + i, near)
        return g, me - core + g // reps, g % reps

    def greet_near(i, c):
        _, t, q = near_peer(i)
        pl.semaphore_signal(barrier, 1, device_id={"rows": t, "rep": q}, device_id_type=MESH)
        return c

    lax.fori_loop(1, reps, greet_near, 0)
    lax.fori_loop(reps + 1, near, greet_near, 0)

    for copy in small:
        copy.wait()

    ids = jnp.concatenate([ids_ref[:, pl.ds(h * width, width)] for h in range(halves)], axis=0)
    owner = ids // items
    local = ids % items
    local_hi = (local // 128).astype(jnp.float32)
    local_lo = (local % 128).astype(jnp.float32)
    lines = ids.shape[0]
    bucket_id = iota((rows, width), 0)
    hits = [(owner[i:i + 1] == bucket_id).astype(jnp.float32) for i in range(lines)]
    before = (iota((width, width), 0) < iota((width, width), 1)).astype(jnp.float32)
    counter = jnp.concatenate([before, jnp.ones((width, width), jnp.float32)], axis=1).astype(jnp.bfloat16)
    counted = dot(jnp.concatenate(hits, axis=0).astype(jnp.bfloat16), counter, ((1,), (0,)), None)
    seen = jnp.zeros((rows, width), jnp.float32)
    ranks = []
    for i in range(lines):
        part = counted[i * rows:(i + 1) * rows]
        ranks.append(jnp.sum(hits[i] * (part[:, :width] + seen), axis=0, keepdims=True))
        seen = seen + part[:, width:]
    rank = jnp.concatenate(ranks, axis=0).astype(jnp.int32)
    pos_v[...] = owner * bucket + rank
    values = jnp.concatenate([jnp.concatenate([hits[i] * local_hi[i:i + 1], hits[i] * local_lo[i:i + 1]], axis=0) for i in range(lines)], axis=1)
    slots = iota((bucket, width), 0)
    picks = jnp.concatenate([(rank[i:i + 1] == slots).astype(jnp.float32) for i in range(lines)], axis=1)
    compact = dot(values.astype(jnp.bfloat16), picks.astype(jnp.bfloat16), ((1,), (1,)), None)
    compact = jnp.clip((compact[:rows] * 128.0 + compact[rows:]).astype(jnp.int32), 0, items - 1)
    for b in range(rows):
        cid[b] = compact[b:b + 1]

    pl.semaphore_wait(barrier, rows - 1 + near - 2)

    def to_row(t, src, dst, which):
        return pltpu.make_async_remote_copy(
            src_ref=src, dst_ref=dst, send_sem=ssem.at[which], recv_sem=rsem.at[which],
            device_id={"rows": t}, device_id_type=MESH)

    def to_rep(q, src, dst, which):
        return pltpu.make_async_remote_copy(
            src_ref=src, dst_ref=dst, send_sem=ssem.at[which], recv_sem=rsem.at[which],
            device_id={"rep": q}, device_id_type=MESH)

    def each_row(fn):
        def go(i, c):
            fn(next_row(i))
            return c

        lax.fori_loop(1, rows, go, 0)

    def each_rep(fn):
        for q in range(1, reps):
            fn(lax.rem(rep + q, reps))

    def drain(sem, ref):
        pltpu.make_async_copy(ref, ref, sem).wait()

    turned = [lax.rem(me // 8 + dz, 4) * 8 for dz in range(4)]
    beside = [lax.rem(me // 2 + dy, 4) * 2 for dy in range(4)]
    stops = (0, 4, 14, 22, rows - 1)
    for d in steps:
        t = turned[d // 8] + beside[d // 2 % 4] + (core if d % 2 == 0 else 1 - core)
        slot = steps.index(opposite(d))
        which = 0 if slot < stops[1] else 1
        pltpu.make_async_remote_copy(
            src_ref=cid.at[t], dst_ref=rid.at[slot], send_sem=id_ssem.at[0], recv_sem=id_rsem.at[which],
            device_id={"rows": t}, device_id_type=MESH).start()
    rid[rows - 1] = cid[me]

    share = quarter // 8

    def add_gram(i, total):
        part = tv[pl.ds(pl.multiple_of(rep * quarter + i * share, share), share), :]
        return total + dot(part, part, ((0,), (0,)))

    table_part(0).wait()
    gpart[...] = lax.fori_loop(0, 8, add_gram, jnp.zeros((width, width), jnp.float32))
    chunk = width // reps

    def chunk_of(q):
        return pl.ds(pl.multiple_of(q * chunk, chunk), chunk)

    each_rep(lambda q: to_rep(q, gpart.at[chunk_of(q)], gx.at[chunk_of(rep)], GRAM_X).start())
    gx[chunk_of(rep), :] = gpart[chunk_of(rep), :]
    for q in range(1, reps):
        table_part(q).wait()

    def fetch(i, dst, base):
        for k in range(bucket):
            dst[pl.ds(base + k, 1), :] = tv[pl.ds(rid_s[i, 0, k], 1), :]

    def take_ids(part, first, last):
        drain(id_rsem.at[part], rid.at[pl.ds(first, min(last, rows - 1) - first)])
        got = pl.ds(first, last - first)
        rid[got] = jnp.clip(rid[got], 0, items - 1)
        copy = pltpu.make_async_copy(rid.at[got], rid_s.at[got], lsem.at[reps])
        copy.start()
        copy.wait()

    def serve(i, t):
        base = pl.multiple_of(t * bucket, bucket)
        fetch(i, sendb, base)
        after = shifted(me, step_of(i + 1))
        at = pl.multiple_of(me * bucket, bucket)
        to_row(t, sendb.at[pl.ds(base, bucket)], recvb.at[pl.ds(at, bucket)], ROWS).start()
        return after

    take_ids(0, 0, stops[1])
    upcoming = shifted(me, jnp.int32(steps[0]))

    def serve_group(g, t):
        return lax.fori_loop(stops[g], stops[g + 1], serve, t)

    upcoming = serve_group(0, upcoming)
    take_ids(1, stops[1], rows)

    drain(rsem.at[GRAM_X], gx.at[pl.ds(0, width - chunk)])
    total = gx[0:chunk, :]
    for q in range(1, reps):
        total = total + gx[q * chunk:(q + 1) * chunk, :]
    for b in range(rows):
        g1[b] = total[b:b + 1]
    each_row(lambda t: to_row(t, g1.at[t], gr.at[me], GRAM_SUM).start())
    gr[me] = g1[me]

    upcoming = serve_group(1, upcoming)

    ub = ub_ref[...]
    home = ub // users
    home_b = jnp.broadcast_to(home, (users, users))
    home_c = jnp.transpose(home_b)
    earlier = iota((users, users), 0) < iota((users, users), 1)
    twin = jnp.sum(jnp.where(earlier & (home_b == home_c), 1.0, 0.0), axis=0, keepdims=True).astype(jnp.int32)
    group = users // near
    far = rows // 2
    home_row, home_rep = home // reps, home % reps
    leave = ((home_row % 2) * reps + home_rep) * group + twin * far + home_row // 2
    hot = (iota((users, users), 0) == leave).astype(jnp.float32)
    place = jnp.sum(hot * (ub % users).astype(jnp.float32), axis=1, keepdims=True)
    place_a[...] = jnp.broadcast_to(place, (users, width))

    def group_of(g):
        return pl.ds(pl.multiple_of(g * group, group), group)

    def leave_near(a, b, which):
        def go(i, c):
            g, t, q = near_peer(i)
            pltpu.make_async_remote_copy(
                src_ref=a.at[group_of(g)], dst_ref=b.at[group_of(here)], send_sem=ssem.at[which], recv_sem=rsem.at[which],
                device_id={"rows": t, "rep": q}, device_id_type=MESH).start()
            return c

        lax.fori_loop(1, near, go, 0)
        b[group_of(here), :] = a[group_of(here), :]

    pieces = users // far
    spot = me // 2

    def piece_of(t):
        return pl.ds(pl.multiple_of(t * pieces, pieces), pieces)

    def leave_far(b, c, d, before, which):
        drain(rsem.at[before], b.at[pl.ds(0, users - group)])
        for t in range(far):
            for j in range(pieces):
                at = t * pieces + j
                c[at:at + 1, :] = b[j * far + t:j * far + t + 1, :]

        def go(i, k):
            t = lax.rem(spot + i, far)
            to_row(2 * t + core, c.at[piece_of(t)], d.at[piece_of(spot)], which).start()
            return k

        lax.fori_loop(1, far, go, 0)
        d[piece_of(spot), :] = c[piece_of(spot), :]

    def arrived(d, which):
        drain(rsem.at[which], d.at[pl.ds(0, users - pieces)])

    leave_near(place_a, place_b, PLACE_NEAR)

    live = iota((length, users), 0) < cnt_ref[...]
    entry = jnp.concatenate([pos_v[h * length:(h + 1) * length, :] for h in range(halves)], axis=1).astype(jnp.float32)
    lists = jnp.concatenate([jnp.where(live, rat_ref[...], 0.0), jnp.where(live, 1.0 + rat_ref[...], 0.0), entry], axis=0)
    lists = dot(lists, hot, ((1,), (1,)))
    w_s[...] = lists[:length]
    pull_s[...] = lists[length:2 * length]
    entry = jnp.concatenate([lists[2 * length:, h * width:(h + 1) * width] for h in range(halves)], axis=0)
    pos_v[...] = jnp.clip(entry.astype(jnp.int32), 0, users * length - 1)
    pos_copy = pltpu.make_async_copy(pos_v, pos_s, lsem.at[reps + 1])
    pos_copy.start()

    drain(rsem.at[GRAM_SUM], gr.at[pl.ds(0, rows - 1)])
    g2[0] = jnp.sum(gr[...], axis=0)
    each_row(lambda t: to_row(t, g2.at[0], gfull.at[rep, me], GRAM_ALL).start())
    gfull[rep, me] = g2[0]

    upcoming = serve_group(2, upcoming)
    drain(rsem.at[GRAM_ALL], gr.at[pl.ds(0, rows - 1)])
    each_rep(lambda q: to_rep(q, gfull.at[rep], gfull.at[rep], GRAM_BACK).start())
    leave_far(place_b, place_c, place_d, PLACE_NEAR, PLACE_FAR)

    upcoming = serve_group(3, upcoming)
    fetch(rows - 1, recvb, pl.multiple_of(me * bucket, bucket))
    drain(rsem.at[GRAM_BACK], gfull.at[pl.ds(0, reps - 1)])
    scale = GRAM_WEIGHT * width / (items * rows)
    for q in range(reps):
        for b in range(rows):
            smat[q * chunk + b:q * chunk + b + 1, :] = gfull[q, b] * scale
    eye = (iota((width, width), 0) == iota((width, width), 1)).astype(jnp.float32)
    smat[...] = smat[...] + REG_WEIGHT * eye

    arrived(place_d, PLACE_FAR)
    place = place_d[...].astype(jnp.int32)
    came = iota((users, width), 0).astype(jnp.float32)
    for h in range(halves):
        here_is = jnp.where(place == iota((users, width), 1) + h * width, came, 0.0)
        inv_v[h:h + 1, :] = jnp.clip(jnp.sum(here_is, axis=0, keepdims=True).astype(jnp.int32), 0, users - 1)
    inv_copy = pltpu.make_async_copy(inv_v, inv_s, lsem.at[0])
    inv_copy.start()
    x_s[...] = jnp.zeros_like(x_s)
    inv_copy.wait()
    pos_copy.wait()
    drain(rsem.at[ROWS], recvb.at[pl.ds(0, (rows - 1) * bucket)])

    def gather(i, dst):
        for k in range(width):
            dst[pl.ds(k, 1), :] = recvb[pl.ds(pos_s[i, k], 1), :]

    def turn(i, c):
        gather(2 * i + 1, blk_b)
        lt[2 * i] = jnp.transpose(blk_a[...])
        gather(jnp.minimum(2 * i + 2, lines - 1), blk_a)
        lt[2 * i + 1] = jnp.transpose(blk_b[...])
        return c

    gather(0, blk_a)
    lax.fori_loop(0, lines // 2, turn, 0)

    for h in range(halves):
        half = slice(h * width, (h + 1) * width)
        rhs = jnp.zeros((width, width), jnp.float32)
        for l in range(length):
            rhs = rhs + lt[h * length + l] * pull_s[l:l + 1, half]
        r_s[:, half] = rhs
        p_s[:, half] = rhs

    def iterate(i, norms):
        q_s[...] = dot(smat[...], p_s[...], ((1,), (0,)))
        out = []
        for h in range(halves):
            half = slice(h * width, (h + 1) * width)
            direc = p_s[:, half]
            image = jnp.zeros((width, width), jnp.float32)
            for l in range(length):
                rows_l = lt[h * length + l]
                proj = jnp.sum(rows_l * direc, axis=0, keepdims=True)
                image = image + rows_l * (w_s[l:l + 1, half] * proj)
            image = image + q_s[:, half]
            alpha = norms[h] / jnp.sum(direc * image, axis=0, keepdims=True)
            x_s[:, half] = x_s[:, half] + alpha * direc
            resid = r_s[:, half] - alpha * image
            r_s[:, half] = resid
            norm_next = jnp.sum(resid * resid, axis=0, keepdims=True)
            p_s[:, half] = resid + norm_next / norms[h] * direc
            out.append(norm_next)
        return tuple(out)

    start = []
    for h in range(halves):
        first = r_s[:, h * width:(h + 1) * width]
        start.append(jnp.sum(first * first, axis=0, keepdims=True))
    lax.fori_loop(0, ITERS, iterate, tuple(start))

    for h in range(halves):
        out_a[h * width:(h + 1) * width, :] = jnp.transpose(x_s[:, h * width:(h + 1) * width])
    leave_near(out_a, out_b, OUT_NEAR)
    leave_far(out_b, out_c, out_d, OUT_NEAR, OUT_FAR)
    arrived(out_d, OUT_FAR)
    for h in range(halves):
        for k in range(width):
            at = h * width + k
            out_ref[at:at + 1, :] = out_d[pl.ds(inv_s[h, k], 1), :]
    result = pltpu.make_async_copy(out_ref, out_hbm, lsem.at[0])
    result.start()

    drain(id_ssem.at[0], cid.at[pl.ds(0, rows - 1)])
    drain(ssem.at[ROWS], sendb.at[pl.ds(0, (rows - 1) * bucket)])
    drain(ssem.at[GRAM_X], gx.at[pl.ds(0, width - chunk)])
    drain(ssem.at[GRAM_SUM], gr.at[pl.ds(0, rows - 1)])
    drain(ssem.at[GRAM_ALL], gr.at[pl.ds(0, rows - 1)])
    drain(ssem.at[GRAM_BACK], gfull.at[pl.ds(0, reps - 1)])
    drain(ssem.at[PLACE_NEAR], place_b.at[pl.ds(0, users - group)])
    drain(ssem.at[PLACE_FAR], place_d.at[pl.ds(0, users - pieces)])
    drain(ssem.at[OUT_NEAR], out_b.at[pl.ds(0, users - group)])
    drain(ssem.at[OUT_FAR], out_d.at[pl.ds(0, users - pieces)])
    result.wait()


def body(rows, reps, item_table, item_ids, ratings, counts, user_batch):
    users, length = item_ids.shape
    items, width = item_table.shape
    slots = users * length
    f32, i32 = jnp.float32, jnp.int32
    hbm = pl.BlockSpec(memory_space=pltpu.HBM)
    square = pltpu.VMEM((width, width), f32)
    wide = pltpu.VMEM((width, users), f32)
    tall = pltpu.VMEM((users, width), f32)
    return pl.pallas_call(
        functools.partial(kernel, rows, reps),
        out_shape=jax.ShapeDtypeStruct((users, width), f32),
        in_specs=[hbm] * 5,
        out_specs=hbm,
        scratch_shapes=[
            pltpu.VMEM((length, users), i32),
            pltpu.VMEM((length, users), f32),
            pltpu.VMEM((1, users), i32),
            pltpu.VMEM((1, users), i32),
            tall,
            pltpu.VMEM((items, width), f32),
            pltpu.VMEM((slots, width), f32),
            pltpu.VMEM((slots, width), f32),
            pltpu.VMEM((slots // width, width, width), f32),
            square, square,
            pltpu.VMEM((rows, 1, width), i32),
            pltpu.VMEM((rows, 1, width), i32),
            pltpu.SMEM((rows, 1, width), i32),
            pltpu.VMEM((slots // width, width), i32),
            pltpu.SMEM((slots // width, width), i32),
            square,
            square,
            pltpu.VMEM((rows, 1, width), f32),
            pltpu.VMEM((rows, 1, width), f32),
            pltpu.VMEM((1, 1, width), f32),
            pltpu.VMEM((reps, rows, 1, width), f32),
            square,
            tall, tall, tall, tall,
            pltpu.VMEM((users // width, width), i32),
            pltpu.SMEM((users // width, width), i32),
            pltpu.VMEM((length, users), f32),
            tall, tall, tall, tall,
            pltpu.VMEM((length, users), f32),
            wide, wide, wide, wide,
            pltpu.SemaphoreType.DMA((9,)),
            pltpu.SemaphoreType.DMA((9,)),
            pltpu.SemaphoreType.DMA((1,)),
            pltpu.SemaphoreType.DMA((2,)),
            pltpu.SemaphoreType.DMA((reps + 6,)),
        ],
        compiler_params=pltpu.CompilerParams(
            collective_id=0, has_side_effects=True, vmem_limit_bytes=63 << 20
        ),
    )(item_ids.T, ratings.T, counts.reshape(1, users), user_batch.reshape(1, users), item_table)


def solution(mesh):
    in_specs = (
        P("rows", None),
        P(("rows", "rep"), None),
        P(("rows", "rep"), None),
        P(("rows", "rep")),
        P(("rows", "rep")),
    )
    out_specs = P(("rows", "rep"), None)
    step = functools.partial(body, mesh.shape["rows"], mesh.shape["rep"])
    return jax.shard_map(step, mesh=mesh, in_specs=in_specs, out_specs=out_specs, check_vma=False)
```

time: 80.3 us -> 62.9 us (0.78)
  Pallas kernels: 73.1 us -> 61.2 us
  local copies, waits for them, and re-layouts: 6.83 us -> 1.57 us
    pallas_call x1, Pallas kernels: 73.1 us -> 61.2 us  [body(): pl.pallas_call(functools.partial(kernel, rows, reps), out_shape=jax.Shape...]
    unnamed x11 -> x1, local copies, waits for them, and re-layouts: 6.83 us -> 1.57 us
where the time goes in v2:
time: 62.9 us; the launch traced here: 62.7 us
  Pallas kernels  61.2 us (97%)
  local copies, waits for them, and re-layouts  1.57 us (2%)
    pallas_call x1, Pallas kernels, body(): pl.pallas_call(functools.partial(kernel, rows, reps), out_shape=jax.Shape...  61.2 us
    unnamed x1, local copies, waits for them, and re-layouts  1.57 us

profile of v2, /device:TPU:1, one launch (start us, length us, event | category | flops | bytes accessed | tf_op | source)
XLA Modules:
  0.0 62.7 jit_solution(8096600599183661347)
XLA Ops:
  0.0 61.2 %shard_map.55 = f32[256,128]{1,0:T(8,128)} custom-call(s32[16,256]{1,0:T(8,128)} %bitcast.4, f32[16,256]{1,0:T(8,128)} %bitcast.5, s32[1,256]{1,0:T(1,128)} %bitcast.6, s32[1,256]{1,0:T(1,128)} %bitcast.7, f32[16384,128]{1,0:T(8,128)} %table_ref.1), custom_call_target="tpu_custom_call" | custom-call | tf_op jit(solution)/shard_map/pallas_call | solution.py:415
  61.2 1.6 %copy.7 = f32[256,128]{1,0:T(8,128)} copy(f32[256,128]{1,0:T(8,128)} %shard_map.55) | data formatting | bytes 262144

commit v3 on v2

--- a/solution.py
+++ b/solution.py
@@ -13,7 +13,7 @@
 HIGH = lax.Precision.HIGHEST
 MESH = pl.DeviceIdType.MESH
 
-ROWS, GRAM_X, PLACE_NEAR, GRAM_SUM, PLACE_FAR, GRAM_ALL, GRAM_BACK, OUT_NEAR, OUT_FAR = range(9)
+ROWS, GRAM_X, PLACE_NEAR, GRAM_SUM, PLACE_FAR, GRAM_ALL, GRAM_BACK, OUT = range(8)
 
 
 def ring_steps(rows):
@@ -46,7 +46,7 @@
     rows, reps, ids_hbm, rat_hbm, cnt_hbm, ub_hbm, table_ref, out_hbm,
     ids_ref, rat_ref, cnt_ref, ub_ref, out_ref, tv, sendb, recvb, lt, blk_a, blk_b, cid, rid, rid_s, pos_v, pos_s,
     gpart, gx, g1, gr, g2, gfull, smat,
-    place_a, place_b, place_c, place_d, inv_v, inv_s, pull_s, out_a, out_b, out_c, out_d,
+    place_a, place_b, place_c, place_d, inv_v, inv_s, pull_s, out_a, out_b, out_d,
     w_s, q_s, x_s, r_s, p_s, ssem, rsem, id_ssem, id_rsem, lsem,
 ):
     me = lax.axis_index("rows")
@@ -241,8 +241,9 @@
     far = rows // 2
     home_row, home_rep = home // reps, home % reps
     leave = ((home_row % 2) * reps + home_rep) * group + twin * far + home_row // 2
-    hot = (iota((users, users), 0) == leave).astype(jnp.float32)
-    place = jnp.sum(hot * (ub % users).astype(jnp.float32), axis=1, keepdims=True)
+    hot = (iota((users, users), 0) == home * 2 + twin).astype(jnp.float32)
+    hot_near = (iota((users, users), 0) == leave).astype(jnp.float32)
+    place = jnp.sum(hot_near * (ub % users).astype(jnp.float32), axis=1, keepdims=True)
     place_a[...] = jnp.broadcast_to(place, (users, width))
 
     def group_of(g):
@@ -380,13 +381,30 @@
 
     for h in range(halves):
         out_a[h * width:(h + 1) * width, :] = jnp.transpose(x_s[:, h * width:(h + 1) * width])
-    leave_near(out_a, out_b, OUT_NEAR)
-    leave_far(out_b, out_c, out_d, OUT_NEAR, OUT_FAR)
-    arrived(out_d, OUT_FAR)
+    devices = rows * reps
+    mine = me * reps + rep
+
+    def pair_of(t):
+        return pl.ds(2 * t, 2)
+
+    def leave_home(i, c):
+        t = mine + i
+        t = jnp.where(t >= devices, t - devices, t)
+        for j in range(2):
+            out_b[2 * t + j] = out_a[pl.ds(2 * t + j, 1), :]
+        pltpu.make_async_remote_copy(
+            src_ref=out_b.at[pair_of(t)], dst_ref=out_d.at[pair_of(mine)], send_sem=ssem.at[OUT], recv_sem=rsem.at[OUT],
+            device_id={"rows": t // reps, "rep": t % reps}, device_id_type=MESH).start()
+        return c
+
+    lax.fori_loop(1, devices, leave_home, 0)
+    for j in range(2):
+        out_d[2 * mine + j] = out_a[pl.ds(2 * mine + j, 1), :]
+    drain(rsem.at[OUT], out_d.at[pl.ds(0, users - 2)])
     for h in range(halves):
         for k in range(width):
             at = h * width + k
-            out_ref[at:at + 1, :] = out_d[pl.ds(inv_s[h, k], 1), :]
+            out_ref[at:at + 1, :] = out_d[inv_s[h, k]]
     result = pltpu.make_async_copy(out_ref, out_hbm, lsem.at[0])
     result.start()
 
@@ -398,8 +416,7 @@
     drain(ssem.at[GRAM_BACK], gfull.at[pl.ds(0, reps - 1)])
     drain(ssem.at[PLACE_NEAR], place_b.at[pl.ds(0, users - group)])
     drain(ssem.at[PLACE_FAR], place_d.at[pl.ds(0, users - pieces)])
-    drain(ssem.at[OUT_NEAR], out_b.at[pl.ds(0, users - group)])
-    drain(ssem.at[OUT_FAR], out_d.at[pl.ds(0, users - pieces)])
+    drain(ssem.at[OUT], out_b.at[pl.ds(0, users - 2)])
     result.wait()
 
 
@@ -411,6 +428,7 @@
     hbm = pl.BlockSpec(memory_space=pltpu.HBM)
     square = pltpu.VMEM((width, width), f32)
     wide = pltpu.VMEM((width, users), f32)
+    single = pltpu.VMEM((users, 1, width), f32)
     tall = pltpu.VMEM((users, width), f32)
     return pl.pallas_call(
         functools.partial(kernel, rows, reps),
@@ -444,11 +462,11 @@
             pltpu.VMEM((users // width, width), i32),
             pltpu.SMEM((users // width, width), i32),
             pltpu.VMEM((length, users), f32),
-            tall, tall, tall, tall,
+            tall, single, single,
             pltpu.VMEM((length, users), f32),
             wide, wide, wide, wide,
-            pltpu.SemaphoreType.DMA((9,)),
-            pltpu.SemaphoreType.DMA((9,)),
+            pltpu.SemaphoreType.DMA((8,)),
+            pltpu.SemaphoreType.DMA((8,)),
             pltpu.SemaphoreType.DMA((1,)),
             pltpu.SemaphoreType.DMA((2,)),
             pltpu.SemaphoreType.DMA((reps + 6,)),

time: 62.9 us -> 62.2 us (0.989)
  Pallas kernels: 61.2 us -> 60.5 us
    pallas_call x1, Pallas kernels: 61.2 us -> 60.5 us  [body(): pl.pallas_call(functools.partial(kernel, rows, reps), out_shape=jax.Shape...]
where the time goes in v3:
time: 62.2 us; the launch traced here: 62.1 us
  Pallas kernels  60.5 us (97%)
  local copies, waits for them, and re-layouts  1.57 us (3%)
    pallas_call x1, Pallas kernels, body(): pl.pallas_call(functools.partial(kernel, rows, reps), out_shape=jax.Shape...  60.5 us
    unnamed x1, local copies, waits for them, and re-layouts  1.57 us

profile of v3, /device:TPU:1, one launch (start us, length us, event | category | flops | bytes accessed | tf_op | source)
XLA Modules:
  0.0 62.1 jit_solution(6908374442053596434)
XLA Ops:
  0.0 60.5 %shard_map.55 = f32[256,128]{1,0:T(8,128)} custom-call(s32[16,256]{1,0:T(8,128)} %bitcast.4, f32[16,256]{1,0:T(8,128)} %bitcast.5, s32[1,256]{1,0:T(1,128)} %bitcast.6, s32[1,256]{1,0:T(1,128)} %bitcast.7, f32[16384,128]{1,0:T(8,128)} %table_ref.1), custom_call_target="tpu_custom_call" | custom-call | tf_op jit(solution)/shard_map/pallas_call | solution.py:433
  60.5 1.6 %copy.7 = f32[256,128]{1,0:T(8,128)} copy(f32[256,128]{1,0:T(8,128)} %shard_map.55) | data formatting | bytes 262144

commit v4 on v3

--- a/solution.py
+++ b/solution.py
@@ -13,13 +13,13 @@
 HIGH = lax.Precision.HIGHEST
 MESH = pl.DeviceIdType.MESH
 
-ROWS, GRAM_X, PLACE_NEAR, GRAM_SUM, PLACE_FAR, GRAM_ALL, GRAM_BACK, OUT = range(8)
+EARLY, LATE, GRAM_X, PLACE_NEAR, GRAM_SUM, PLACE_FAR, GRAM_ALL, GRAM_BACK, OUT = range(9)
 
 
 def ring_steps(rows):
     def hops(d):
         dy, dz = (d // 2) % 4, d // 8
-        return min(dy, 4 - dy) + min(dz, 4 - dz)
+        return min(dy, 4 - dy) + min(dz, 4 - dz) or 1.5
 
     return sorted(range(1, rows), key=lambda d: (-hops(d), d % 2))
 
@@ -38,14 +38,19 @@
     return lax.dot_general(a, b, (dims, ((), ())), precision=precision, preferred_element_type=jnp.float32)
 
 
+def halve(a):
+    high = a.astype(jnp.bfloat16)
+    return high, (a - high.astype(jnp.float32)).astype(jnp.bfloat16)
+
+
 def iota(shape, axis):
     return lax.broadcasted_iota(jnp.int32, shape, axis)
 
 
 def kernel(
     rows, reps, ids_hbm, rat_hbm, cnt_hbm, ub_hbm, table_ref, out_hbm,
-    ids_ref, rat_ref, cnt_ref, ub_ref, out_ref, tv, sendb, recvb, lt, blk_a, blk_b, cid, rid, rid_s, pos_v, pos_s,
-    gpart, gx, g1, gr, g2, gfull, smat,
+    ids_ref, rat_ref, cnt_ref, ub_ref, out_ref, tv, sendb, earlyb, lateb, late_v, late_hot, late_turned, lt, blk_a, blk_b, cid, rid, rid_s, pos_v, pos_s,
+    gpart, gx, g1, gr, g2, gfull, smat, smat3,
     place_a, place_b, place_c, place_d, inv_v, inv_s, pull_s, out_a, out_b, out_d,
     w_s, q_s, x_s, r_s, p_s, ssem, rsem, id_ssem, id_rsem, lsem,
 ):
@@ -59,11 +64,21 @@
     halves = users // width
     steps = ring_steps(rows)
 
+    def pick(i, values):
+        d = jnp.int32(values[0])
+        for k in range(1, len(values)):
+            d = jnp.where(i == k, values[k], d)
+        return d
+
     def step_of(i):
-        d = jnp.int32(steps[0])
-        for k in range(1, len(steps)):
-            d = jnp.where(i == k, steps[k], d)
-        return d
+        return pick(i, steps)
+
+    meets = [steps.index(opposite(d)) for d in steps]
+    stops = (0, 4, 14, rows - 9, rows - 1)
+    first_late = stops[3]
+    own_slot = first_late
+    zero_row = (own_slot + 1) * bucket
+    late_rows = (rows - 1 - first_late) * bucket
 
     def table_part(q):
         at = pl.multiple_of(lax.rem(rep + q, reps) * quarter, quarter)
@@ -163,7 +178,6 @@
 
     turned = [lax.rem(me // 8 + dz, 4) * 8 for dz in range(4)]
     beside = [lax.rem(me // 2 + dy, 4) * 2 for dy in range(4)]
-    stops = (0, 4, 14, 22, rows - 1)
     for d in steps:
         t = turned[d // 8] + beside[d // 2 % 4] + (core if d % 2 == 0 else 1 - core)
         slot = steps.index(opposite(d))
@@ -175,12 +189,12 @@
 
     share = quarter // 8
 
-    def add_gram(i, total):
+    table_part(0).wait()
+    gram = jnp.zeros((width, width), jnp.float32)
+    for i in range(8):
         part = tv[pl.ds(pl.multiple_of(rep * quarter + i * share, share), share), :]
-        return total + dot(part, part, ((0,), (0,)))
-
-    table_part(0).wait()
-    gpart[...] = lax.fori_loop(0, 8, add_gram, jnp.zeros((width, width), jnp.float32))
+        gram = gram + dot(part, part, ((0,), (0,)))
+    gpart[...] = gram
     chunk = width // reps
 
     def chunk_of(q):
@@ -203,19 +217,24 @@
         copy.start()
         copy.wait()
 
-    def serve(i, t):
-        base = pl.multiple_of(t * bucket, bucket)
-        fetch(i, sendb, base)
-        after = shifted(me, step_of(i + 1))
-        at = pl.multiple_of(me * bucket, bucket)
-        to_row(t, sendb.at[pl.ds(base, bucket)], recvb.at[pl.ds(at, bucket)], ROWS).start()
-        return after
+    def serve(late):
+        def go(i, t):
+            base = pl.multiple_of(t * bucket, bucket)
+            fetch(i, sendb, base)
+            after = shifted(me, step_of(i + 1))
+            slot = pick(i, meets) - (first_late if late else 0)
+            at = pl.multiple_of(slot * bucket, bucket)
+            dst = lateb if late else earlyb
+            to_row(t, sendb.at[pl.ds(base, bucket)], dst.at[pl.ds(at, bucket)], LATE if late else EARLY).start()
+            return after
+
+        return go
 
     take_ids(0, 0, stops[1])
     upcoming = shifted(me, jnp.int32(steps[0]))
 
     def serve_group(g, t):
-        return lax.fori_loop(stops[g], stops[g + 1], serve, t)
+        return lax.fori_loop(stops[g], stops[g + 1], serve(g == 3), t)
 
     upcoming = serve_group(0, upcoming)
     take_ids(1, stops[1], rows)
@@ -289,13 +308,23 @@
     live = iota((length, users), 0) < cnt_ref[...]
     entry = jnp.concatenate([pos_v[h * length:(h + 1) * length, :] for h in range(halves)], axis=1).astype(jnp.float32)
     lists = jnp.concatenate([jnp.where(live, rat_ref[...], 0.0), jnp.where(live, 1.0 + rat_ref[...], 0.0), entry], axis=0)
-    lists = dot(lists, hot, ((1,), (1,)))
+    lists = dot(jnp.concatenate(halve(lists), axis=0), hot.astype(jnp.bfloat16), ((1,), (1,)), None)
+    lists = lists[:3 * length] + lists[3 * length:]
     w_s[...] = lists[:length]
     pull_s[...] = lists[length:2 * length]
     entry = jnp.concatenate([lists[2 * length:, h * width:(h + 1) * width] for h in range(halves)], axis=0)
-    pos_v[...] = jnp.clip(entry.astype(jnp.int32), 0, users * length - 1)
+    entry = jnp.clip(entry.astype(jnp.int32), 0, users * length - 1)
+    holder = entry // bucket
+    slot = jnp.full(holder.shape, own_slot, jnp.int32)
+    for i, d in enumerate(steps):
+        t = turned[d // 8] + beside[d // 2 % 4] + (core if d % 2 == 0 else 1 - core)
+        slot = jnp.where(holder == t, i if i < first_late else i + 1, slot)
+    entry = slot * bucket + entry % bucket
+    late_v[...] = entry - zero_row
+    pos_v[...] = jnp.minimum(entry, zero_row)
     pos_copy = pltpu.make_async_copy(pos_v, pos_s, lsem.at[reps + 1])
     pos_copy.start()
+    earlyb[pl.ds(zero_row, 8), :] = jnp.zeros((8, width), jnp.float32)
 
     drain(rsem.at[GRAM_SUM], gr.at[pl.ds(0, rows - 1)])
     g2[0] = jnp.sum(gr[...], axis=0)
@@ -303,19 +332,46 @@
     gfull[rep, me] = g2[0]
 
     upcoming = serve_group(2, upcoming)
+
+    upcoming = serve_group(3, upcoming)
+    fetch(rows - 1, earlyb, own_slot * bucket)
+    def mark(b, c):
+        for u in range(2):
+            want = late_v[pl.ds(2 * b + u, 1), :]
+            late_hot[b, :, u * width:(u + 1) * width] = (iota((late_rows, width), 0) == want).astype(jnp.float32).astype(jnp.bfloat16)
+        return c
+
+    lax.fori_loop(0, lines // 2, mark, 0)
     drain(rsem.at[GRAM_ALL], gr.at[pl.ds(0, rows - 1)])
     each_rep(lambda q: to_rep(q, gfull.at[rep], gfull.at[rep], GRAM_BACK).start())
     leave_far(place_b, place_c, place_d, PLACE_NEAR, PLACE_FAR)
 
-    upcoming = serve_group(3, upcoming)
-    fetch(rows - 1, recvb, pl.multiple_of(me * bucket, bucket))
+    pos_copy.wait()
+    drain(rsem.at[EARLY], earlyb.at[pl.ds(0, first_late * bucket)])
+
+    def gather(i, dst):
+        for k in range(width):
+            dst[pl.ds(k, 1), :] = earlyb[pl.ds(pos_s[i, k], 1), :]
+
+    def turn(i, c):
+        gather(2 * i + 1, blk_b)
+        lt[2 * i] = jnp.transpose(blk_a[...])
+        gather(jnp.minimum(2 * i + 2, lines - 1), blk_a)
+        lt[2 * i + 1] = jnp.transpose(blk_b[...])
+        return c
+
+    gather(0, blk_a)
+    lax.fori_loop(0, lines // 2, turn, 0)
+
     drain(rsem.at[GRAM_BACK], gfull.at[pl.ds(0, reps - 1)])
     scale = GRAM_WEIGHT * width / (items * rows)
     for q in range(reps):
         for b in range(rows):
             smat[q * chunk + b:q * chunk + b + 1, :] = gfull[q, b] * scale
     eye = (iota((width, width), 0) == iota((width, width), 1)).astype(jnp.float32)
-    smat[...] = smat[...] + REG_WEIGHT * eye
+    smat_hi, smat_lo = halve(smat[...] + REG_WEIGHT * eye)
+    for k, piece in enumerate((smat_hi, smat_lo, smat_hi)):
+        smat3[:, k * width:(k + 1) * width] = piece
 
     arrived(place_d, PLACE_FAR)
     place = place_d[...].astype(jnp.int32)
@@ -327,22 +383,17 @@
     inv_copy.start()
     x_s[...] = jnp.zeros_like(x_s)
     inv_copy.wait()
-    pos_copy.wait()
-    drain(rsem.at[ROWS], recvb.at[pl.ds(0, (rows - 1) * bucket)])
-
-    def gather(i, dst):
-        for k in range(width):
-            dst[pl.ds(k, 1), :] = recvb[pl.ds(pos_s[i, k], 1), :]
-
-    def turn(i, c):
-        gather(2 * i + 1, blk_b)
-        lt[2 * i] = jnp.transpose(blk_a[...])
-        gather(jnp.minimum(2 * i + 2, lines - 1), blk_a)
-        lt[2 * i + 1] = jnp.transpose(blk_b[...])
-        return c
-
-    gather(0, blk_a)
-    lax.fori_loop(0, lines // 2, turn, 0)
+    drain(rsem.at[LATE], lateb)
+    for c in range(late_rows // width):
+        columns = slice(c * width, (c + 1) * width)
+        late_hi, late_lo = halve(jnp.transpose(lateb[columns, :]))
+        late_turned[:width, columns] = late_hi
+        late_turned[width:, columns] = late_lo
+    for b in range(lines // 2):
+        more = dot(late_turned[...], late_hot[b], ((1,), (0,)), None)
+        for u in range(2):
+            columns = slice(u * width, (u + 1) * width)
+            lt[2 * b + u] = lt[2 * b + u] + more[:width, columns] + more[width:, columns]
 
     for h in range(halves):
         half = slice(h * width, (h + 1) * width)
@@ -353,7 +404,8 @@
         p_s[:, half] = rhs
 
     def iterate(i, norms):
-        q_s[...] = dot(smat[...], p_s[...], ((1,), (0,)))
+        p_hi, p_lo = halve(p_s[...])
+        q_s[...] = dot(smat3[...], jnp.concatenate([p_hi, p_hi, p_lo], axis=0), ((1,), (0,)), None)
         out = []
         for h in range(halves):
             half = slice(h * width, (h + 1) * width)
@@ -409,7 +461,8 @@
     result.start()
 
     drain(id_ssem.at[0], cid.at[pl.ds(0, rows - 1)])
-    drain(ssem.at[ROWS], sendb.at[pl.ds(0, (rows - 1) * bucket)])
+    drain(ssem.at[EARLY], sendb.at[pl.ds(0, first_late * bucket)])
+    drain(ssem.at[LATE], sendb.at[pl.ds(0, late_rows)])
     drain(ssem.at[GRAM_X], gx.at[pl.ds(0, width - chunk)])
     drain(ssem.at[GRAM_SUM], gr.at[pl.ds(0, rows - 1)])
     drain(ssem.at[GRAM_ALL], gr.at[pl.ds(0, rows - 1)])
@@ -424,7 +477,8 @@
     users, length = item_ids.shape
     items, width = item_table.shape
     slots = users * length
-    f32, i32 = jnp.float32, jnp.int32
+    f32, i32, bf16 = jnp.float32, jnp.int32, jnp.bfloat16
+    late = 8 * (slots // rows)
     hbm = pl.BlockSpec(memory_space=pltpu.HBM)
     square = pltpu.VMEM((width, width), f32)
     wide = pltpu.VMEM((width, users), f32)
@@ -443,7 +497,11 @@
             tall,
             pltpu.VMEM((items, width), f32),
             pltpu.VMEM((slots, width), f32),
-            pltpu.VMEM((slots, width), f32),
+            pltpu.VMEM((slots - late + 8, width), f32),
+            pltpu.VMEM((late, width), f32),
+            pltpu.VMEM((slots // width, width), i32),
+            pltpu.VMEM((slots // width // 2, late, 2 * width), bf16),
+            pltpu.VMEM((2 * width, late), bf16),
             pltpu.VMEM((slots // width, width, width), f32),
             square, square,
             pltpu.VMEM((rows, 1, width), i32),
@@ -458,6 +516,7 @@
             pltpu.VMEM((1, 1, width), f32),
             pltpu.VMEM((reps, rows, 1, width), f32),
             square,
+            pltpu.VMEM((width, 3 * width), bf16),
             tall, tall, tall, tall,
             pltpu.VMEM((users // width, width), i32),
             pltpu.SMEM((users // width, width), i32),
@@ -465,8 +524,8 @@
             tall, single, single,
             pltpu.VMEM((length, users), f32),
             wide, wide, wide, wide,
-            pltpu.SemaphoreType.DMA((8,)),
-            pltpu.SemaphoreType.DMA((8,)),
+            pltpu.SemaphoreType.DMA((9,)),
+            pltpu.SemaphoreType.DMA((9,)),
             pltpu.SemaphoreType.DMA((1,)),
             pltpu.SemaphoreType.DMA((2,)),
             pltpu.SemaphoreType.DMA((reps + 6,)),

time: 62.2 us -> 59.1 us (0.950)
  Pallas kernels: 60.5 us -> 57.4 us
    pallas_call x1, Pallas kernels: 60.5 us -> 57.4 us  [body(): pl.pallas_call(functools.partial(kernel, rows, reps), out_shape=jax.Shape...]
where the time goes in v4:
time: 59.1 us; the launch traced here: 58.9 us
  Pallas kernels  57.4 us (97%)
  local copies, waits for them, and re-layouts  1.57 us (3%)
    pallas_call x1, Pallas kernels, body(): pl.pallas_call(functools.partial(kernel, rows, reps), out_shape=jax.Shape...  57.4 us
    unnamed x1, local copies, waits for them, and re-layouts  1.57 us

profile of v4, /device:TPU:1, one launch (start us, length us, event | category | flops | bytes accessed | tf_op | source)
XLA Modules:
  0.0 58.9 jit_solution(1624960105144559601)
XLA Ops:
  0.0 57.4 %shard_map.55 = f32[256,128]{1,0:T(8,128)} custom-call(s32[16,256]{1,0:T(8,128)} %bitcast.4, f32[16,256]{1,0:T(8,128)} %bitcast.5, s32[1,256]{1,0:T(1,128)} %bitcast.6, s32[1,256]{1,0:T(1,128)} %bitcast.7, f32[16384,128]{1,0:T(8,128)} %table_ref.1), custom_call_target="tpu_custom_call" | custom-call | tf_op jit(solution)/shard_map/pallas_call | solution.py:487
  57.4 1.6 %copy.7 = f32[256,128]{1,0:T(8,128)} copy(f32[256,128]{1,0:T(8,128)} %shard_map.55) | data formatting | bytes 262144

commit v5 on v4

--- a/solution.py
+++ b/solution.py
@@ -52,7 +52,7 @@
     ids_ref, rat_ref, cnt_ref, ub_ref, out_ref, tv, sendb, earlyb, lateb, late_v, late_hot, late_turned, lt, blk_a, blk_b, cid, rid, rid_s, pos_v, pos_s,
     gpart, gx, g1, gr, g2, gfull, smat, smat3,
     place_a, place_b, place_c, place_d, inv_v, inv_s, pull_s, out_a, out_b, out_d,
-    w_s, q_s, x_s, r_s, p_s, ssem, rsem, id_ssem, id_rsem, lsem,
+    w_s, x_s, r_s, p_s, ssem, rsem, id_ssem, id_rsem, lsem,
 ):
     me = lax.axis_index("rows")
     rep = lax.axis_index("rep")
@@ -403,33 +403,30 @@
         r_s[:, half] = rhs
         p_s[:, half] = rhs
 
-    def iterate(i, norms):
-        p_hi, p_lo = halve(p_s[...])
-        q_s[...] = dot(smat3[...], jnp.concatenate([p_hi, p_hi, p_lo], axis=0), ((1,), (0,)), None)
-        out = []
+    norms = []
+    for h in range(halves):
+        first = r_s[:, h * width:(h + 1) * width]
+        norms.append(jnp.sum(first * first, axis=0, keepdims=True))
+    for step in range(ITERS):
         for h in range(halves):
             half = slice(h * width, (h + 1) * width)
             direc = p_s[:, half]
+            p_hi, p_lo = halve(direc)
+            spread = dot(smat3[...], jnp.concatenate([p_hi, p_hi, p_lo], axis=0), ((1,), (0,)), None)
             image = jnp.zeros((width, width), jnp.float32)
             for l in range(length):
                 rows_l = lt[h * length + l]
                 proj = jnp.sum(rows_l * direc, axis=0, keepdims=True)
                 image = image + rows_l * (w_s[l:l + 1, half] * proj)
-            image = image + q_s[:, half]
+            image = image + spread
             alpha = norms[h] / jnp.sum(direc * image, axis=0, keepdims=True)
             x_s[:, half] = x_s[:, half] + alpha * direc
-            resid = r_s[:, half] - alpha * image
-            r_s[:, half] = resid
-            norm_next = jnp.sum(resid * resid, axis=0, keepdims=True)
-            p_s[:, half] = resid + norm_next / norms[h] * direc
-            out.append(norm_next)
-        return tuple(out)
-
-    start = []
-    for h in range(halves):
-        first = r_s[:, h * width:(h + 1) * width]
-        start.append(jnp.sum(first * first, axis=0, keepdims=True))
-    lax.fori_loop(0, ITERS, iterate, tuple(start))
+            if step < ITERS - 1:
+                resid = r_s[:, half] - alpha * image
+                r_s[:, half] = resid
+                norm_next = jnp.sum(resid * resid, axis=0, keepdims=True)
+                p_s[:, half] = resid + norm_next / norms[h] * direc
+                norms[h] = norm_next
 
     for h in range(halves):
         out_a[h * width:(h + 1) * width, :] = jnp.transpose(x_s[:, h * width:(h + 1) * width])
@@ -523,7 +520,7 @@
             pltpu.VMEM((length, users), f32),
             tall, single, single,
             pltpu.VMEM((length, users), f32),
-            wide, wide, wide, wide,
+            wide, wide, wide,
             pltpu.SemaphoreType.DMA((9,)),
             pltpu.SemaphoreType.DMA((9,)),
             pltpu.SemaphoreType.DMA((1,)),

time: 59.1 us -> 58.3 us (0.986)
  Pallas kernels: 57.4 us -> 56.6 us
    pallas_call x1, Pallas kernels: 57.4 us -> 56.6 us  [body(): pl.pallas_call(functools.partial(kernel, rows, reps), out_shape=jax.Shape...]
where the time goes in v5:
time: 58.3 us; the launch traced here: 58.2 us
  Pallas kernels  56.6 us (97%)
  local copies, waits for them, and re-layouts  1.57 us (3%)
    pallas_call x1, Pallas kernels, body(): pl.pallas_call(functools.partial(kernel, rows, reps), out_shape=jax.Shape...  56.6 us
    unnamed x1, local copies, waits for them, and re-layouts  1.57 us

profile of v5, /device:TPU:1, one launch (start us, length us, event | category | flops | bytes accessed | tf_op | source)
XLA Modules:
  0.0 58.2 jit_solution(12305309491970454063)
XLA Ops:
  0.0 56.6 %shard_map.55 = f32[256,128]{1,0:T(8,128)} custom-call(s32[16,256]{1,0:T(8,128)} %bitcast.4, f32[16,256]{1,0:T(8,128)} %bitcast.5, s32[1,256]{1,0:T(1,128)} %bitcast.6, s32[1,256]{1,0:T(1,128)} %bitcast.7, f32[16384,128]{1,0:T(8,128)} %table_ref.1), custom_call_target="tpu_custom_call" | custom-call | tf_op jit(solution)/shard_map/pallas_call | solution.py:484
  56.6 1.6 %copy.7 = f32[256,128]{1,0:T(8,128)} copy(f32[256,128]{1,0:T(8,128)} %shard_map.55) | data formatting | bytes 262144

commit v6 on v5

--- a/solution.py
+++ b/solution.py
@@ -74,7 +74,7 @@
         return pick(i, steps)
 
     meets = [steps.index(opposite(d)) for d in steps]
-    stops = (0, 4, 14, rows - 9, rows - 1)
+    stops = (0, 4, 17, rows - 9, rows - 1)
     first_late = stops[3]
     own_slot = first_late
     zero_row = (own_slot + 1) * bucket
@@ -450,12 +450,16 @@
     for j in range(2):
         out_d[2 * mine + j] = out_a[pl.ds(2 * mine + j, 1), :]
     drain(rsem.at[OUT], out_d.at[pl.ds(0, users - 2)])
+
+    def result_part(h):
+        part = pl.ds(h * width, width)
+        return pltpu.make_async_copy(out_ref.at[part], out_hbm.at[part], lsem.at[h])
+
     for h in range(halves):
         for k in range(width):
             at = h * width + k
             out_ref[at:at + 1, :] = out_d[inv_s[h, k]]
-    result = pltpu.make_async_copy(out_ref, out_hbm, lsem.at[0])
-    result.start()
+        result_part(h).start()
 
     drain(id_ssem.at[0], cid.at[pl.ds(0, rows - 1)])
     drain(ssem.at[EARLY], sendb.at[pl.ds(0, first_late * bucket)])
@@ -467,7 +471,8 @@
     drain(ssem.at[PLACE_NEAR], place_b.at[pl.ds(0, users - group)])
     drain(ssem.at[PLACE_FAR], place_d.at[pl.ds(0, users - pieces)])
     drain(ssem.at[OUT], out_b.at[pl.ds(0, users - 2)])
-    result.wait()
+    for h in range(halves):
+        result_part(h).wait()
 
 
 def body(rows, reps, item_table, item_ids, ratings, counts, user_batch):

time: 58.3 us -> 58.1 us (level)
  no operation moved by 1% of the time
where the time goes in v6:
time: 58.1 us; the launch traced here: 58 us
  Pallas kernels  56.4 us (97%)
  local copies, waits for them, and re-layouts  1.57 us (3%)
    pallas_call x1, Pallas kernels, body(): pl.pallas_call(functools.partial(kernel, rows, reps), out_shape=jax.Shape...  56.4 us
    unnamed x1, local copies, waits for them, and re-layouts  1.57 us

profile of v6, /device:TPU:1, one launch (start us, length us, event | category | flops | bytes accessed | tf_op | source)
XLA Modules:
  0.0 58.0 jit_solution(14775801856370349703)
XLA Ops:
  0.0 56.4 %shard_map.55 = f32[256,128]{1,0:T(8,128)} custom-call(s32[16,256]{1,0:T(8,128)} %bitcast.4, f32[16,256]{1,0:T(8,128)} %bitcast.5, s32[1,256]{1,0:T(1,128)} %bitcast.6, s32[1,256]{1,0:T(1,128)} %bitcast.7, f32[16384,128]{1,0:T(8,128)} %table_ref.1), custom_call_target="tpu_custom_call" | custom-call | tf_op jit(solution)/shard_map/pallas_call | solution.py:489
  56.4 1.6 %copy.7 = f32[256,128]{1,0:T(8,128)} copy(f32[256,128]{1,0:T(8,128)} %shard_map.55) | data formatting | bytes 262144
